TPU v7x, 256 devices: a whole 4x4x8 slice. The times are simulated.
256 devices in a mesh: prow: 16 (over y_lo, z), pcol: 16 (over x, y_hi, core).
Axes of the slice: x: 4, y: 4 (y_hi: 2, y_lo: 2; y = y_hi * 2 + y_lo), z: 8, core: 2. Of those that a mesh axis runs over, the one named last changes fastest.
Arguments:
- ancestor_inverse: bfloat16 [12288, 12288], P('pcol', 'prow'), may hold values from -0.0546875 to 0.0546875
- factor_panel: bfloat16 [3, 12288, 1024], P(None, 'prow', 'pcol'), may hold values from -1.5 to 1.5
- pattern: int32 [3, 96], replicated, may hold values 0 or 1
- diagonal_inverse: float32 [3, 1024, 1024], P(None, 'pcol', 'prow'), may hold values from -6 to 6
Outputs:
- offdiag_inverse: float32 [3, 12288, 1024], P(None, 'pcol', 'prow')
- diagonal_block: float32 [3, 1024, 1024], P(None, 'pcol', 'prow')
All inputs are finite; a program needn't handle non-finite values.
Results may differ from a plain program's by a relative error of at most 0.0003.
Values may be sent and summed in bfloat16 or wider, within the bound.
No kernel may reach another device: no remote copies, remote signals or barrier semaphores. Data moves between devices by JAX's collectives and lax.ppermute only.
A program may use at most 128 MiB of HBM per device.

v0:
```python
import jax
import jax.numpy as jnp
from jax import lax
from jax.sharding import PartitionSpec as P

BLK = 128


def spread_2(value, axis, source):
    kept = jnp.where(lax.axis_index(axis) == source, value, 0).astype(value.dtype)
    return lax.psum(kept, axis)


def local_mask(pattern, first, count, block):
    picked = lax.dynamic_slice_in_dim(pattern, first, count, 1)
    spread = jnp.broadcast_to(picked[:, :, None], (picked.shape[0], count, block))
    return spread.reshape(picked.shape[0], count * block)


def selected_step(ancestor_inverse, masked, mask_cols, diag_term):
    row_panel = lax.all_gather(masked, "pcol", axis=2, tiled=True)
    partial_value = jnp.einsum(
        "ij,kjn->kin", ancestor_inverse, row_panel, preferred_element_type=jnp.float32
    )
    group_ratio = lax.axis_size("prow") // lax.axis_size("pcol")
    col_index = lax.axis_index("pcol")
    pieces = spread_2(row_panel, "prow", col_index * group_ratio + 0)
    col_panel = pieces.astype(jnp.float32)
    reduced = lax.psum_scatter(partial_value, "prow", scatter_dimension=2, tiled=True)
    offdiag = -(reduced * mask_cols[:, :, None])
    square = jnp.einsum("kin,kim->knm", col_panel, offdiag, precision=lax.Precision.HIGHEST)
    diagonal = diag_term - lax.psum_scatter(square, "pcol", scatter_dimension=1, tiled=True)
    return (offdiag, diagonal)


def shards(ancestor_inverse, factor_panel, pattern, diagonal_inverse):
    per_prow = factor_panel.shape[1] // BLK
    per_pcol = ancestor_inverse.shape[0] // BLK
    mask_rows = local_mask(pattern, lax.axis_index("prow") * per_prow, per_prow, BLK).astype(
        jnp.bfloat16
    )
    mask_cols = local_mask(pattern, lax.axis_index("pcol") * per_pcol, per_pcol, BLK).astype(
        jnp.float32
    )
    masked = factor_panel * mask_rows[:, :, None]
    offdiag, diagonal = selected_step(ancestor_inverse, masked, mask_cols, diagonal_inverse)
    return (offdiag, diagonal)


def solution(mesh):
    in_specs = (P("pcol", "prow"), P(None, "prow", "pcol"), P(), P(None, "pcol", "prow"))
    out_specs = (P(None, "pcol", "prow"), P(None, "pcol", "prow"))
    return jax.shard_map(shards, mesh=mesh, in_specs=in_specs, out_specs=out_specs, check_vma=False)
```

profile of v0, /device:TPU:2, one launch (start us, length us, event | category | flops | bytes accessed | tf_op | source)
XLA Modules:
  0.0 442.0 jit_solution(10268001574837307801)
XLA Ops:
  7.2 0.0 copy-start
  7.2 0.0 all-gather.2.cloned.1.call-start
  7.2 0.9 dynamic-slice_convert_fusion
  8.1 0.1 broadcast_bitcast_fusion.1
  8.2 1.7 broadcast_multiply_fusion
  9.9 0.0 all-gather.2.cloned.1.call-update
  9.9 0.0 reduce-scatter.3.cloned.1.call-start
  10.0 67.2 %all-gather.2.cloned.1.call-done = bf16[3,768,1024]{1,2,0:T(8,128)(2,1)} async-done(((bf16[3,768,64]{1,2,0:T(8,128)(2,1)}), bf16[3,768,1024]{1,2,0:T(8,128)(2,1)}) %all-gather.2.cloned.1.call-update) | async-done | bytes 4718608 | tf_op jit(solution)/shard_map/all_gather | solution.py:21
  77.1 0.0 copy-done
  77.1 8.8 %convolution_bitcast_fusion = f32[3,768,1024]{1,2,0:T(8,128)} fusion(bf16[3,768,1024]{1,2,0:T(8,128)(2,1)} %all-gather.2.cloned.1.call-done, bf16[768,768]{1,0:T(8,128)(2,1)S(1)} %copy-done), kind=kOutput, calls=%fused_computation.1 | convolution fusion | flops 3623878656 | bytes 15335424 | tf_op jit(solution)/shard_map/ij,kjn->kin/dot_general | solution.py:22
  85.9 0.0 reduce-scatter.3.cloned.1.call-update
  85.9 0.0 all-reduce.2.cloned.1.call-start
  86.0 2.4 broadcast_select_fusion
  88.4 0.0 all-reduce.2.cloned.1.call-update
  88.4 0.0 reduce-scatter.5.cloned.1.call-start
  88.5 0.1 broadcast_bitcast_fusion
  88.6 108.3 %reduce-scatter.3.cloned.1.call-done = f32[3,768,64]{1,2,0:T(8,128)} async-done(((f32[3,768,1024]{1,2,0:T(8,128)}), f32[3,768,64]{1,2,0:T(8,128)}) %reduce-scatter.3.cloned.1.call-update) | async-done | bytes 589840 | tf_op jit(solution)/shard_map/reduce_scatter | solution.py:29
  196.9 0.0 copy-start.2
  196.9 1.1 multiply_negate_fusion
  198.1 0.0 copy-start.1
  198.1 155.0 %all-reduce.2.cloned.1.call-done = bf16[3,768,1024]{1,2,0:T(8,128)(2,1)} async-done(((bf16[3,768,1024]{1,2,0:T(8,128)(2,1)}), bf16[3,768,1024]{1,2,0:T(8,128)(2,1)}) %all-reduce.2.cloned.1.call-update) | async-done | bytes 4718608 | tf_op jit(solution)/shard_map/psum | solution.py:11
  353.1 7.3 %fusion.1 = f32[3,1024,64]{2,1,0:T(8,128)} fusion(bf16[3,768,1024]{1,2,0:T(8,128)(2,1)} %all-reduce.2.cloned.1.call-done, f32[3,768,64]{1,2,0:T(8,128)S(1)} %multiply_negate_fusion), kind=kOutput, calls=%fused_computation.11 | convolution fusion | flops 1811939328 | bytes 6094848 | tf_op jit(solution)/shard_map/kin,kim->knm/dot_general | solution.py:31
  360.4 0.0 reduce-scatter.5.cloned.1.call-update
  360.4 73.5 %reduce-scatter.5.cloned.1.call-done = f32[3,64,64]{2,1,0:T(8,128)} async-done(((f32[3,1024,64]{2,1,0:T(8,128)}), f32[3,64,64]{2,1,0:T(8,128)}) %reduce-scatter.5.cloned.1.call-update) | async-done | bytes 49168 | tf_op jit(solution)/shard_map/reduce_scatter | solution.py:32
  433.9 0.0 copy-done.2
  433.9 1.5 sub.3
  435.5 0.0 copy-done.1
  (2 shorter events, 0.0 us)
Async XLA Ops:
  7.2 70.0 %copy-start = (bf16[768,768]{1,0:T(8,128)(2,1)S(1)}, bf16[768,768]{1,0:T(8,128)(2,1)}, u32[]{:S(2)}) copy-start(bf16[768,768]{1,0:T(8,128)(2,1)} %param.4) | copy-start | bytes 3538948
  7.2 70.0 %all-gather.2.cloned.1.call-start = ((), (), s32[]{:S(2)}) async-start(), calls=%async_computation.2 | async-start | bytes 5013504 | tf_op jit(solution)/shard_map/all_gather | solution.py:21
  9.9 187.0 %reduce-scatter.3.cloned.1.call-start = ((), (), s32[]{:S(2)}) async-start(), calls=%async_computation.3 | async-start | bytes 10027008 | tf_op jit(solution)/shard_map/reduce_scatter | solution.py:29
  85.9 267.2 %all-reduce.2.cloned.1.call-start = ((), (), s32[]{:S(2)}) async-start(), calls=%async_computation.4 | async-start | bytes 9437184 | tf_op jit(solution)/shard_map/psum | solution.py:11
  88.4 345.5 %reduce-scatter.5.cloned.1.call-start = ((), (), s32[]{:S(2)}) async-start(), calls=%async_computation.5 | async-start | bytes 1671168 | tf_op jit(solution)/shard_map/reduce_scatter | solution.py:32
  196.9 237.0 %copy-start.2 = (f32[3,64,64]{2,1,0:T(8,128)S(1)}, f32[3,64,64]{2,1,0:T(8,128)}, u32[]{:S(2)}) copy-start(f32[3,64,64]{2,1,0:T(8,128)} %param.7) | copy-start | bytes 147460
  198.1 237.4 %copy-start.1 = (f32[3,768,64]{1,2,0:T(8,128)}, f32[3,768,64]{1,2,0:T(8,128)S(1)}, u32[]{:S(2)}) copy-start(f32[3,768,64]{1,2,0:T(8,128)S(1)} %multiply_negate_fusion) | copy-start | bytes 1769476
Sparse Core Ops, SparseCore 0:
  11.4 65.7 all-gather.1
  86.0 110.8 reduce-scatter.2
  199.6 153.4 all-reduce.1
  360.5 73.3 reduce-scatter.4
where the time goes:
time: 442 us
  waiting for transfers between devices  404 us (91%)
  matrix products  16.1 us (4%)
  between operations  13.8 us (3%)
  other arithmetic  7.69 us (2%)
    psum x1, waiting for transfers between devices, spread_2(): return lax.psum(kept, axis)  155 us
    reduce_scatter x1, waiting for transfers between devices, selected_step(): lax.psum_scatter(partial_value, 'prow', scatter_dimension=2, tiled=True)  108 us
    reduce_scatter x1, waiting for transfers between devices, selected_step(): lax.psum_scatter(square, 'pcol', scatter_dimension=1, tiled=True)  73.5 us
    all_gather x1, waiting for transfers between devices, selected_step(): row_panel = lax.all_gather(masked, 'pcol', axis=2, tiled=True)  67.2 us
  transfers between devices with their start and end apart: 4, of which 4 were waited for; matrix products, arithmetic and copies ran while one was open for 1% of the time, Pallas kernels for 0%

commit v1 on v0

--- a/solution.py
+++ b/solution.py
@@ -4,11 +4,12 @@
 from jax.sharding import PartitionSpec as P
 
 BLK = 128
+_extend_pairs_all = lambda values, chip_axis: jnp.sum(lax.all_gather(values, chip_axis), 0)
 
 
 def spread_2(value, axis, source):
     kept = jnp.where(lax.axis_index(axis) == source, value, 0).astype(value.dtype)
-    return lax.psum(kept, axis)
+    return _extend_pairs_all(kept, axis)
 
 
 def local_mask(pattern, first, count, block):

time: 442 us -> 1090 us (2.47)
  waiting for transfers between devices: 404 us -> 1020 us
  other arithmetic: 7.69 us -> 34.3 us
    all_gather x0 -> x1, waiting for transfers between devices: none -> 774 us  [lax.all_gather(values, chip_axis)]
    psum x1 -> x0, waiting for transfers between devices: 155 us -> none  [spread_2(): return lax.psum(kept, axis)]
    reduce_sum x0 -> x1, other arithmetic: none -> 26.6 us  [jnp.sum(lax.all_gather(values, chip_axis), 0)]
where the time goes in v1:
time: 1090 us
  waiting for transfers between devices  1020 us (94%)
  other arithmetic  34.3 us (3%)
  matrix products  16.6 us (2%)
  between operations  13.8 us (1%)
    all_gather x1, waiting for transfers between devices, lax.all_gather(values, chip_axis)  774 us
    reduce_scatter x1, waiting for transfers between devices, selected_step(): lax.psum_scatter(partial_value, 'prow', scatter_dimension=2, tiled=True)  102 us
    reduce_scatter x1, waiting for transfers between devices, selected_step(): lax.psum_scatter(square, 'pcol', scatter_dimension=1, tiled=True)  74 us
    all_gather x1, waiting for transfers between devices, selected_step(): row_panel = lax.all_gather(masked, 'pcol', axis=2, tiled=True)  67.2 us
    reduce_sum x1, other arithmetic, jnp.sum(lax.all_gather(values, chip_axis), 0)  26.6 us
  transfers between devices with their start and end apart: 4, of which 4 were waited for; matrix products, arithmetic and copies ran while one was open for 1% of the time, Pallas kernels for 0%

profile of v1, /device:TPU:2, one launch (start us, length us, event | category | flops | bytes accessed | tf_op | source)
XLA Modules:
  0.0 1088.1 jit_solution(16596551547738697070)
XLA Ops:
  7.2 0.0 copy-start
  7.2 0.0 all-gather.4.cloned.1.call-start
  7.2 0.9 dynamic-slice_convert_fusion
  8.1 0.1 broadcast_bitcast_fusion.1
  8.2 1.7 broadcast_multiply_fusion
  9.9 0.0 all-gather.4.cloned.1.call-update
  9.9 0.0 reduce-scatter.3.cloned.1.call-start
  10.0 67.2 %all-gather.4.cloned.1.call-done = bf16[3,768,1024]{1,2,0:T(8,128)(2,1)} async-done(((bf16[3,768,64]{1,2,0:T(8,128)(2,1)}), bf16[3,768,1024]{1,2,0:T(8,128)(2,1)}) %all-gather.4.cloned.1.call-update) | async-done | bytes 4718608 | tf_op jit(solution)/shard_map/all_gather | solution.py:22
  77.1 0.0 copy-done
  77.1 8.7 convolution_bitcast_fusion
  85.9 0.0 reduce-scatter.3.cloned.1.call-update
  85.9 0.0 all-gather.6.cloned.1.call-start
  86.0 2.5 broadcast_select_fusion
  88.4 6.6 copy.7
  95.1 0.0 all-gather.6.cloned.1.call-update
  95.1 0.0 reduce-scatter.5.cloned.1.call-start
  95.1 0.1 broadcast_bitcast_fusion
  95.2 101.7 %reduce-scatter.3.cloned.1.call-done = f32[3,768,64]{1,2,0:T(8,128)} async-done(((f32[3,768,1024]{1,2,0:T(8,128)}), f32[3,768,64]{1,2,0:T(8,128)}) %reduce-scatter.3.cloned.1.call-update) | async-done | bytes 589840 | tf_op jit(solution)/shard_map/reduce_scatter | solution.py:30
  196.9 1.1 multiply_negate_fusion
  198.0 0.0 copy-start.1
  198.0 773.5 %all-gather.6.cloned.1.call-done = bf16[48,768,1024]{2,1,0:T(8,128)(2,1)} async-done(((bf16[3,768,1024]{2,1,0:T(8,128)(2,1)}), bf16[48,768,1024]{2,1,0:T(8,128)(2,1)}) %all-gather.6.cloned.1.call-update) | async-done | bytes 75497488 | tf_op jit(solution)/shard_map/all_gather | solution.py:7
  971.5 26.6 %reduce_sum.12 = bf16[3,768,1024]{2,1,0:T(8,128)(2,1)} reduce(bf16[16,3,768,1024]{3,2,1,0:T(8,128)(2,1)} %bitcast.2, bf16[]{:T(256)} %constant.16.clone.1), dimensions={0}, to_apply=%region_1.2 | reduce | flops 35389440 | bytes 80216064 | tf_op jit(solution)/shard_map/reduce_sum | solution.py:7
  998.1 0.0 copy-done.1
  998.1 0.0 copy-start.2
  998.1 7.8 fusion.1
  1005.9 0.0 reduce-scatter.5.cloned.1.call-update
  1006.0 74.0 %reduce-scatter.5.cloned.1.call-done = f32[3,64,64]{2,1,0:T(8,128)} async-done(((f32[3,1024,64]{2,1,0:T(8,128)}), f32[3,64,64]{2,1,0:T(8,128)}) %reduce-scatter.5.cloned.1.call-update) | async-done | bytes 49168 | tf_op jit(solution)/shard_map/reduce_scatter | solution.py:33
  1080.0 0.0 copy-done.2
  1080.0 1.5 sub.3
  (2 shorter events, 0.0 us)
Async XLA Ops:
  7.2 70.0 %copy-start = (bf16[768,768]{1,0:T(8,128)(2,1)S(1)}, bf16[768,768]{1,0:T(8,128)(2,1)}, u32[]{:S(2)}) copy-start(bf16[768,768]{1,0:T(8,128)(2,1)} %param.4) | copy-start | bytes 3538948
  7.2 70.0 %all-gather.4.cloned.1.call-start = ((), (), s32[]{:S(2)}) async-start(), calls=%async_computation.2 | async-start | bytes 5013504 | tf_op jit(solution)/shard_map/all_gather | solution.py:22
  9.9 187.0 %reduce-scatter.3.cloned.1.call-start = ((), (), s32[]{:S(2)}) async-start(), calls=%async_computation.3 | async-start | bytes 10027008 | tf_op jit(solution)/shard_map/reduce_scatter | solution.py:30
  85.9 885.6 %all-gather.6.cloned.1.call-start = ((), (), s32[]{:S(2)}) async-start(), calls=%async_computation.5 | async-start | bytes 80216064 | tf_op jit(solution)/shard_map/all_gather | solution.py:7
  95.1 984.9 %reduce-scatter.5.cloned.1.call-start = ((), (), s32[]{:S(2)}) async-start(), calls=%async_computation.4 | async-start | bytes 1671168 | tf_op jit(solution)/shard_map/reduce_scatter | solution.py:33
  198.0 800.1 %copy-start.1 = (f32[3,768,64]{1,2,0:T(8,128)}, f32[3,768,64]{1,2,0:T(8,128)S(1)}, u32[]{:S(2)}) copy-start(f32[3,768,64]{1,2,0:T(8,128)S(1)} %multiply_negate_fusion) | copy-start | bytes 1769476
  998.1 81.9 %copy-start.2 = (f32[3,64,64]{2,1,0:T(8,128)S(1)}, f32[3,64,64]{2,1,0:T(8,128)}, u32[]{:S(2)}) copy-start(f32[3,64,64]{2,1,0:T(8,128)} %param.7) | copy-start | bytes 147460
Sparse Core Ops, SparseCore 0:
  11.4 65.7 all-gather.3
  86.0 110.8 reduce-scatter.2
  198.7 772.7 all-gather.5
  1006.1 73.8 reduce-scatter.4

commit v2 on v0

--- a/solution.py
+++ b/solution.py
@@ -4,6 +4,11 @@
 from jax.sharding import PartitionSpec as P
 
 BLK = 128
+
+
+def exchange_gather(x, name, along):
+    stack = jnp.stack([x] * lax.axis_size(name))
+    return jnp.concatenate(lax.all_to_all(stack, name, 0, 0), axis=along)
 
 
 def spread_2(value, axis, source):
@@ -18,7 +23,7 @@
 
 
 def selected_step(ancestor_inverse, masked, mask_cols, diag_term):
-    row_panel = lax.all_gather(masked, "pcol", axis=2, tiled=True)
+    row_panel = exchange_gather(masked, "pcol", 2)
     partial_value = jnp.einsum(
         "ij,kjn->kin", ancestor_inverse, row_panel, preferred_element_type=jnp.float32
     )

time: 442 us -> 439 us (level)
  waiting for transfers between devices: 404 us -> 336 us
  blocking collectives: 0 us -> 62.2 us
    all_gather x1 -> x0, waiting for transfers between devices: 67.2 us -> none  [selected_step(): row_panel = lax.all_gather(masked, 'pcol', axis=2, tiled=True)]
    all_to_all x0 -> x1, blocking collectives: none -> 62.2 us  [exchange_gather(): return jnp.concatenate(lax.all_to_all(stack, name, 0, 0), axis=along)]
  transfers between devices with their start and end apart: 4 -> 3, of which waited for: 4 -> 3; matrix products, arithmetic and copies ran while one was open for 1% -> 1% of each run, Pallas kernels for 0% -> 0%
where the time goes in v2:
time: 439 us
  waiting for transfers between devices  336 us (77%)
  blocking collectives  62.2 us (14%)
  between operations  13.8 us (3%)
  matrix products  13.7 us (3%)
  other arithmetic  9.3 us (2%)
    psum x1, waiting for transfers between devices, spread_2(): return lax.psum(kept, axis)  155 us
    reduce_scatter x1, waiting for transfers between devices, selected_step(): lax.psum_scatter(partial_value, 'prow', scatter_dimension=2, tiled=True)  107 us
    reduce_scatter x1, waiting for transfers between devices, selected_step(): lax.psum_scatter(square, 'pcol', scatter_dimension=1, tiled=True)  73.5 us
    all_to_all x1, blocking collectives, exchange_gather(): return jnp.concatenate(lax.all_to_all(stack, name, 0, 0), axis=along)  62.2 us
  transfers between devices with their start and end apart: 3, of which 3 were waited for; matrix products, arithmetic and copies ran while one was open for 1% of the time, Pallas kernels for 0%

profile of v2, /device:TPU:2, one launch (start us, length us, event | category | flops | bytes accessed | tf_op | source)
XLA Modules:
  0.0 438.7 jit_solution(17746654641403492135)
XLA Ops:
  7.2 0.0 copy-start
  7.2 0.0 reduce-scatter.3.cloned.1.call-start
  7.2 0.9 dynamic-slice_convert_fusion
  8.1 0.1 broadcast_bitcast_fusion.1
  8.2 1.0 broadcast_multiply_fusion
  9.2 0.6 stack.2
  9.7 62.2 %all_to_all.5 = bf16[16,3,768,64]{2,3,1,0:T(8,128)(2,1)S(1)} all-to-all(bf16[16,3,768,64]{2,3,1,0:T(8,128)(2,1)S(1)} %stack.2), channel_id=1, replica_groups=mesh['prow'=16,'pcol'=16] {'pcol'}, dimensions={0} | all-to-all | bytes 9437184 | tf_op jit(solution)/shard_map/all_to_all | solution.py:11
  71.9 0.5 copy.6
  72.5 0.0 copy-start.1
  72.5 2.2 copy-done.1
  74.7 0.0 copy-done
  74.7 6.4 %convolution_bitcast_fusion = f32[3,768,1024]{1,2,0:T(8,128)} fusion(bf16[3,768,1024]{1,2,0:T(8,128)(2,1)S(1)} %bitcast.21, bf16[768,768]{1,0:T(8,128)(2,1)S(1)} %copy-done), kind=kOutput, calls=%fused_computation.1 | convolution fusion | flops 3623878656 | bytes 15335424 | tf_op jit(solution)/shard_map/ij,kjn->kin/dot_general | solution.py:27
  81.1 0.0 reduce-scatter.3.cloned.1.call-update
  81.2 0.0 all-reduce.2.cloned.1.call-start
  81.2 4.8 %broadcast_select_fusion = bf16[3,768,1024]{1,2,0:T(8,128)(2,1)} fusion(pred[]{:T(512)S(6)} %eq.3, bf16[3,768,16,64]{1,3,2,0:T(8,128)(2,1)} %copy-done.1), kind=kLoop, calls=%fused_computation | loop fusion | flops 2359296 | bytes 9437185 | tf_op jit(solution)/shard_map/jit(_where)/select_n | solution.py:15
  86.0 0.0 all-reduce.2.cloned.1.call-update
  86.0 0.0 reduce-scatter.5.cloned.1.call-start
  86.1 0.1 broadcast_bitcast_fusion
  86.1 107.5 %reduce-scatter.3.cloned.1.call-done = f32[3,768,64]{1,2,0:T(8,128)} async-done(((f32[3,768,1024]{1,2,0:T(8,128)}), f32[3,768,64]{1,2,0:T(8,128)}) %reduce-scatter.3.cloned.1.call-update) | async-done | bytes 589840 | tf_op jit(solution)/shard_map/reduce_scatter | solution.py:34
  193.6 0.0 copy-start.3
  193.6 1.1 multiply_negate_fusion
  194.8 0.0 copy-start.2
  194.8 154.9 %all-reduce.2.cloned.1.call-done = bf16[3,768,1024]{1,2,0:T(8,128)(2,1)} async-done(((bf16[3,768,1024]{1,2,0:T(8,128)(2,1)}), bf16[3,768,1024]{1,2,0:T(8,128)(2,1)}) %all-reduce.2.cloned.1.call-update) | async-done | bytes 4718608 | tf_op jit(solution)/shard_map/psum | solution.py:16
  349.7 7.3 %fusion.1 = f32[3,1024,64]{2,1,0:T(8,128)} fusion(bf16[3,768,1024]{1,2,0:T(8,128)(2,1)} %all-reduce.2.cloned.1.call-done, f32[3,768,64]{1,2,0:T(8,128)S(1)} %multiply_negate_fusion), kind=kOutput, calls=%fused_computation.11 | convolution fusion | flops 1811939328 | bytes 6094848 | tf_op jit(solution)/shard_map/kin,kim->knm/dot_general | solution.py:36
  357.0 0.0 reduce-scatter.5.cloned.1.call-update
  357.1 73.5 %reduce-scatter.5.cloned.1.call-done = f32[3,64,64]{2,1,0:T(8,128)} async-done(((f32[3,1024,64]{2,1,0:T(8,128)}), f32[3,64,64]{2,1,0:T(8,128)}) %reduce-scatter.5.cloned.1.call-update) | async-done | bytes 49168 | tf_op jit(solution)/shard_map/reduce_scatter | solution.py:37
  430.6 0.0 copy-done.3
  430.6 1.5 sub.3
  432.1 0.0 copy-done.2
  (2 shorter events, 0.0 us)
Async XLA Ops:
  7.2 67.5 %copy-start = (bf16[768,768]{1,0:T(8,128)(2,1)S(1)}, bf16[768,768]{1,0:T(8,128)(2,1)}, u32[]{:S(2)}) copy-start(bf16[768,768]{1,0:T(8,128)(2,1)} %param.4) | copy-start | bytes 3538948
  7.2 186.4 %reduce-scatter.3.cloned.1.call-start = ((), (), s32[]{:S(2)}) async-start(), calls=%async_computation.3 | async-start | bytes 10027008 | tf_op jit(solution)/shard_map/reduce_scatter | solution.py:34
  72.5 2.2 copy-start.1
  81.2 268.6 %all-reduce.2.cloned.1.call-start = ((), (), s32[]{:S(2)}) async-start(), calls=%async_computation.4 | async-start | bytes 9437184 | tf_op jit(solution)/shard_map/psum | solution.py:16
  86.0 344.6 %reduce-scatter.5.cloned.1.call-start = ((), (), s32[]{:S(2)}) async-start(), calls=%async_computation.5 | async-start | bytes 1671168 | tf_op jit(solution)/shard_map/reduce_scatter | solution.py:37
  193.6 237.0 %copy-start.3 = (f32[3,64,64]{2,1,0:T(8,128)S(1)}, f32[3,64,64]{2,1,0:T(8,128)}, u32[]{:S(2)}) copy-start(f32[3,64,64]{2,1,0:T(8,128)} %param.7) | copy-start | bytes 147460
  194.8 237.4 %copy-start.2 = (f32[3,768,64]{1,2,0:T(8,128)}, f32[3,768,64]{1,2,0:T(8,128)S(1)}, u32[]{:S(2)}) copy-start(f32[3,768,64]{1,2,0:T(8,128)S(1)} %multiply_negate_fusion) | copy-start | bytes 1769476
Sparse Core Ops, SparseCore 0:
  81.3 112.2 reduce-scatter.2
  196.3 153.3 all-reduce.1
  357.2 73.3 reduce-scatter.4
